TPU v7x, 32 devices: a whole 2x2x4 slice. The times are simulated.
32 devices in a mesh: pairs: 2 (over x), tgt: 16 (over z, y, core).
Axes of the slice: x: 2, y: 2, z: 4, core: 2. Of those that a mesh axis runs over, the one named last changes fastest.
Arguments:
- src_hidden: bfloat16 [4096, 128], P(('pairs', 'tgt')), parts along dimension 0, may hold values from -6 to 6
- tgt_hidden: bfloat16 [256, 256, 128], P(('pairs', 'tgt')), parts along dimension 0, may hold values from -6 to 6
- proj_weight: bfloat16 [128, 256], replicated, may hold values from -0.5 to 0.5
- proj_bias: float32 [256], replicated, may hold values from -1.5 to 1.5
Outputs:
- level_one: bfloat16 [128, 128, 2048], P(('pairs', 'tgt')), parts along dimension 0
- level_two: bfloat16 [4096, 2048], P(('pairs', 'tgt')), parts along dimension 0
- level_three: bfloat16 [4096, 512], P(('pairs', 'tgt')), parts along dimension 0
There are 2 independent parts, one for each index of `pairs`. A program takes and returns all parts, laid end to end along the dimension named above; an argument that names none is the same for every part. Nothing has to cross between parts.
All inputs are finite; a program needn't handle non-finite values.
Results may differ from a plain program's by a relative error of at most 0.006.
Values may be sent and summed in bfloat16 or wider, within the bound.
A program may use at most 64 MiB of HBM per device.

v0:
```python
import math
import jax
import jax.numpy as jnp
from jax import lax
from jax.sharding import PartitionSpec as P


def project_features(hidden, weight, bias):
    result = jnp.dot(hidden, weight, preferred_element_type=jnp.float32) + bias
    return result.astype(jnp.bfloat16)


def pool_leading(values):
    height, across, depth = values.shape
    return values.reshape(height // 2, 2, across // 2, 2, depth).mean(axis=(1, 3))


def pool_trailing(values):
    depth, height, across = values.shape
    return values.reshape(depth, height // 2, 2, across // 2, 2).mean(axis=(2, 4))


def split_parts(values):
    upper = values.astype(jnp.bfloat16)
    lower = (values - upper.astype(jnp.float32)).astype(jnp.bfloat16)
    return (upper, lower)


def per_device(src_hidden, tgt_hidden, proj_weight, proj_bias):
    row_count, col_count, hidden_width = tgt_hidden.shape
    channels = proj_weight.shape[1]
    stripe_count = lax.axis_size("tgt")
    own_sources = src_hidden.shape[0]
    source_count = own_sources * stripe_count
    inverse_root = 1.0 / math.sqrt(channels)
    tgt_feat = project_features(
        tgt_hidden.reshape(row_count * col_count, hidden_width), proj_weight, proj_bias
    )
    grid_feat = tgt_feat.astype(jnp.float32).reshape(row_count, col_count, channels)
    fine_pool = pool_leading(grid_feat)
    coarse_pool = pool_leading(fine_pool)
    fine_upper, fine_lower = split_parts(fine_pool.reshape(-1, channels))
    coarse_upper, coarse_lower = split_parts(coarse_pool.reshape(-1, channels))
    own_features = project_features(src_hidden, proj_weight, proj_bias)
    all_features = lax.all_gather(own_features, "tgt", axis=0, tiled=True)
    block_size = 512
    block_total = source_count // block_size
    fine_count = fine_upper.shape[0]
    coarse_count = coarse_upper.shape[0]
    empty_levels = (
        jnp.zeros((fine_count, source_count), jnp.bfloat16),
        jnp.zeros((source_count, coarse_count), jnp.bfloat16),
    )
    contract_last = (((1,), (1,)), ((), ()))

    def one_block(block_index, levels):
        level_one, coarse_rows = levels
        offset = (block_index * block_size).astype(jnp.int32)
        panel = lax.dynamic_slice_in_dim(all_features, offset, block_size, 0)
        fine_corr = lax.dot_general(
            fine_upper, panel, contract_last, preferred_element_type=jnp.float32
        )
        fine_corr = fine_corr + lax.dot_general(
            fine_lower, panel, contract_last, preferred_element_type=jnp.float32
        )
        coarse_corr = lax.dot_general(
            panel, coarse_upper, contract_last, preferred_element_type=jnp.float32
        )
        coarse_corr = coarse_corr + lax.dot_general(
            panel, coarse_lower, contract_last, preferred_element_type=jnp.float32
        )
        zero_index = jnp.zeros((), jnp.int32)
        level_one = lax.dynamic_update_slice(
            level_one, (fine_corr * inverse_root).astype(jnp.bfloat16), (zero_index, offset)
        )
        coarse_rows = lax.dynamic_update_slice(
            coarse_rows, (coarse_corr * inverse_root).astype(jnp.bfloat16), (offset, zero_index)
        )
        return (level_one, coarse_rows)

    level_one, coarse_rows = lax.fori_loop(0, block_total, one_block, empty_levels)
    level_one = level_one.reshape(row_count // 2, col_count // 2, source_count)
    level_two = lax.all_to_all(coarse_rows, "tgt", split_axis=0, concat_axis=1, tiled=True)
    coarse_grid = level_two.astype(jnp.float32).reshape(
        own_sources, stripe_count * (row_count // 4), col_count // 4
    )
    level_three = pool_trailing(coarse_grid).reshape(own_sources, -1).astype(jnp.bfloat16)
    return (level_one, level_two, level_three)


def solution(mesh):
    return jax.shard_map(
        per_device,
        mesh=mesh,
        in_specs=(P(("pairs", "tgt"), None), P(("pairs", "tgt"), None, None), P(), P()),
        out_specs=(
            P(("pairs", "tgt"), None, None),
            P(("pairs", "tgt"), None),
            P(("pairs", "tgt"), None),
        ),
        check_vma=False,
    )
```

profile of v0, /device:TPU:0, one launch (start us, length us, event | category | flops | bytes accessed | tf_op | source)
XLA Modules:
  0.0 93.0 jit_solution(4818545377180773034)
XLA Ops:
  7.2 1.7 %fusion.18 = bf16[128,256]{1,0:T(8,128)(2,1)} fusion(bf16[128,128]{1,0:T(8,128)(2,1)} %param.6, bf16[128,256]{1,0:T(8,128)(2,1)} %param.8, f32[256]{0:T(256)} %param.9), kind=kOutput, calls=%fused_computation.23 | convolution fusion | flops 8454144 | bytes 164864 | tf_op jit(solution)/shard_map/dot_general | solution.py:9
  8.9 2.6 %fusion.17 = f32[2048,256]{1,0:T(8,128)} fusion(bf16[2048,128]{1,0:T(8,128)(2,1)S(1)} %bitcast.40, bf16[128,256]{1,0:T(8,128)(2,1)} %param.8, f32[256]{0:T(256)} %param.9), kind=kOutput, calls=%fused_computation.21 | convolution fusion | flops 135790592 | bytes 2688000 | tf_op jit(solution)/shard_map/dot_general | solution.py:9
  11.5 2.5 %reshape.38 = f32[4,2,128,2,256]{4,3,2,1,0:T(2,128)S(1)} reshape(f32[2048,256]{1,0:T(8,128)} %fusion.17) | data formatting | bytes 4194304 | tf_op jit(solution)/shard_map/reshape;reshape | solution.py:15
  14.0 1.5 %reduce_sum.27 = f32[4,128,256]{2,1,0:T(8,128)S(1)} reduce(f32[4,2,128,2,256]{4,3,2,1,0:T(2,128)S(1)} %reshape.38, f32[]{:T(128)} %constant.47.clone.1), dimensions={1,3}, to_apply=%region_0.0 | reduce | flops 393216 | bytes 2621444 | tf_op jit(solution)/shard_map/reduce_sum | solution.py:15
  15.5 0.3 div.27
  15.9 0.4 reduce_sum.28
  16.3 35.1 %all-gather.2.cloned.1.call-done = bf16[2048,256]{1,0:T(8,128)(2,1)} async-done(((bf16[128,256]{1,0:T(8,128)(2,1)}), bf16[2048,256]{1,0:T(8,128)(2,1)}) %all-gather.2.cloned.1.call-update) | async-done | bytes 1048592 | tf_op jit(solution)/shard_map/all_gather | solution.py:45
  51.4 0.9 broadcast_in_dim.9
  52.3 1.6 %broadcast_in_dim.8.clone = bf16[512,2048]{1,0:T(8,128)(2,1)} broadcast(bf16[]{:T(256)} %constant.46.clone.1), dimensions={} | broadcast | bytes 2097154 | tf_op jit(solution)/shard_map/broadcast_in_dim | solution.py:51
  53.9 11.4 %while.15 = (s32[]{:T(128)}, bf16[512,2048]{1,0:T(8,128)(2,1)}, bf16[2048,128]{1,0:T(8,128)(2,1)}, bf16[2048,256]{1,0:T(8,128)(2,1)S(1)}, bf16[512,256]{1,0:T(8,...) while((s32[]{:T(128)}, bf16[512,2048]{1,0:T(8,128)(2,1)}, ...), condition=%wide.region_3.0_spmd, body=%wide.region_2.0_spmd.sunk | while | flops 336527360 | bytes 7079091 | solution.py:81
  54.1 0.9 fusion.52
  55.0 0.3 fusion.49
  55.3 0.3 fusion.50
  55.9 0.8 constant_dynamic-update-slice_fusion.2
  56.9 0.9 fusion.52
  57.8 0.3 fusion.49
  58.2 0.3 fusion.50
  58.7 0.8 constant_dynamic-update-slice_fusion.2
  59.5 0.2 fusion.51
  59.8 0.9 fusion.52
  60.7 0.3 fusion.49
  61.0 0.3 fusion.50
  61.5 0.8 constant_dynamic-update-slice_fusion.2
  62.6 0.9 fusion.52
  63.5 0.3 fusion.49
  63.8 0.3 fusion.50
  64.4 0.8 constant_dynamic-update-slice_fusion.2
  65.2 18.1 %all_to_all.19 = bf16[16,128,128]{2,1,0:T(8,128)(2,1)S(1)} all-to-all(bf16[16,128,128]{2,1,0:T(8,128)(2,1)} %bitcast.5), channel_id=1, replica_groups=mesh['pairs'=2,'tgt'=16] {'tgt'}, dimensions={0} | all-to-all | bytes 1048576 | tf_op jit(solution)/shard_map/all_to_all | solution.py:83
  83.3 0.3 copy.22
  83.6 1.0 %copy.25 = bf16[128,2048]{1,0:T(8,128)(2,1)} copy(bf16[128,2048]{0,1:T(8,128)(2,1)S(1)} %bitcast.44) | data formatting | bytes 1048576
  84.7 0.5 copy.23
  85.4 0.8 copy.26
  (21 shorter events, 1.9 us)
Async XLA Ops:
  7.2 1.8 %copy-start = (bf16[8,256,128]{2,1,0:T(8,128)(2,1)S(1)}, bf16[8,256,128]{2,1,0:T(8,128)(2,1)}, u32[]{:S(2)}) copy-start(bf16[8,256,128]{2,1,0:T(8,128)(2,1)} %param.7) | copy-start | bytes 1572868
  7.2 44.2 %all-gather.2.cloned.1.call-start = ((), (), s32[]{:S(2)}) async-start(), calls=%async_computation.1 | async-start | bytes 1114112 | tf_op jit(solution)/shard_map/all_gather | solution.py:45
  51.4 2.4 %copy-start.1 = (bf16[2048,256]{1,0:T(8,128)(2,1)S(1)}, bf16[2048,256]{1,0:T(8,128)(2,1)}, u32[]{:S(2)}) copy-start(bf16[2048,256]{1,0:T(8,128)(2,1)} %all-gather.2.cloned.1.call-done) | copy-start | bytes 3145732
Sparse Core Ops, SparseCore 0:
  10.8 40.6 all-gather.1
where the time goes:
time: 93.3 us; the launch traced here: 93 us
  waiting for transfers between devices  35.1 us (38%)
  blocking collectives  18.1 us (19%)
  between operations  14.2 us (15%)
  local copies, waits for them, and re-layouts  12 us (13%)
  matrix products  11.3 us (12%)
  other arithmetic  2.17 us (2%)
    all_gather x1, waiting for transfers between devices, per_device(): all_features = lax.all_gather(own_features, 'tgt', axis=0, tiled=True)  35.1 us
    all_to_all x1, blocking collectives, per_device(): lax.all_to_all(coarse_rows, 'tgt', split_axis=0, concat_axis=1, tiled=True)  18.1 us
    dot_general x2, matrix products, project_features(): result = jnp.dot(hidden, weight, preferred_element_type=jnp.float32) + bias  4.25 us
    dynamic_update_slice x8, local copies, waits for them, and re-layouts, one_block(): lax.dynamic_update_slice(level_one, (fine_corr * inverse_root).astype(jnp...  4.19 us
    dot_general x4, matrix products, one_block(): lax.dot_general(panel, coarse_lower, contract_last, preferred_element_typ...  3.57 us
    another operation x1, local copies, waits for them, and re-layouts, pool_leading(): values.reshape(height // 2, 2, across // 2, 2, depth).mean(axis=(1, 3))  2.49 us
  transfers between devices with their start and end apart: 1, of which 1 were waited for; matrix products, arithmetic and copies ran while one was open for 8% of the time, Pallas kernels for 0%

commit v1 on v0

--- a/solution.py
+++ b/solution.py
@@ -42,7 +42,18 @@
     fine_upper, fine_lower = split_parts(fine_pool.reshape(-1, channels))
     coarse_upper, coarse_lower = split_parts(coarse_pool.reshape(-1, channels))
     own_features = project_features(src_hidden, proj_weight, proj_bias)
-    all_features = lax.all_gather(own_features, "tgt", axis=0, tiled=True)
+    length, index, rows = (lax.axis_size("tgt"), lax.axis_index("tgt"), own_features.shape[0])
+    right = [(i, (i + 1) % length) for i in range(length)]
+    out = jnp.zeros(
+        (*own_features.shape[:0], length * rows, *own_features.shape[0 + 1 :]), own_features.dtype
+    )
+    block = own_features
+    for turn in range(length):
+        owner = (index - turn) % length
+        out = lax.dynamic_update_slice_in_dim(out, block, owner * rows, axis=0)
+        if turn < length - 1:
+            block = lax.ppermute(block, "tgt", right)
+    all_features = out
     block_size = 512
     block_total = source_count // block_size
     fine_count = fine_upper.shape[0]

time: 93.3 us -> 138 us (1.48)
  waiting for transfers between devices: 35.1 us -> 87.2 us
  between operations: 14.2 us -> 1.17 us
  starting transfers between devices: 0.04 us -> 3.23 us
  other arithmetic: 2.17 us -> 3.79 us
    ppermute x0 -> x15, waiting for transfers between devices: none -> 87.2 us  [per_device(): block = lax.ppermute(block, 'tgt', right)]
    all_gather x1 -> x0, waiting for transfers between devices: 35.1 us -> none  [per_device(): all_features = lax.all_gather(own_features, 'tgt', axis=0, tiled=True)]
    ppermute x0 -> x15, starting transfers between devices: none -> 3.23 us  [per_device(): block = lax.ppermute(block, 'tgt', right)]
    reduce_sum x2, other arithmetic: 1.84 us -> 3.46 us  [pool_leading(): values.reshape(height // 2, 2, across // 2, 2, depth).mean(axis=(1, 3))]
  transfers between devices with their start and end apart: 1 -> 15, of which waited for: 1 -> 14; matrix products, arithmetic and copies ran while one was open for 8% -> 7% of each run, Pallas kernels for 0% -> 0%
where the time goes in v1:
time: 138 us; the launch traced here: 137 us
  waiting for transfers between devices  87.2 us (63%)
  blocking collectives  18 us (13%)
  local copies, waits for them, and re-layouts  13.2 us (10%)
  matrix products  10.7 us (8%)
  other arithmetic  3.79 us (3%)
  starting transfers between devices  3.23 us (2%)
    ppermute x15, waiting for transfers between devices, per_device(): block = lax.ppermute(block, 'tgt', right)  87.2 us
    all_to_all x1, blocking collectives, per_device(): lax.all_to_all(coarse_rows, 'tgt', split_axis=0, concat_axis=1, tiled=True)  18 us
    dynamic_update_slice x8, local copies, waits for them, and re-layouts, one_block(): lax.dynamic_update_slice(level_one, (fine_corr * inverse_root).astype(jnp...  4.19 us
    dot_general x2, matrix products, project_features(): result = jnp.dot(hidden, weight, preferred_element_type=jnp.float32) + bias  3.61 us
    dot_general x4, matrix products, one_block(): lax.dot_general(panel, coarse_lower, contract_last, preferred_element_typ...  3.56 us
    another operation x1, local copies, waits for them, and re-layouts, pool_leading(): values.reshape(height // 2, 2, across // 2, 2, depth).mean(axis=(1, 3))  3.47 us
    reduce_sum x2, other arithmetic, pool_leading(): values.reshape(height // 2, 2, across // 2, 2, depth).mean(axis=(1, 3))  3.46 us
    ppermute x15, starting transfers between devices, per_device(): block = lax.ppermute(block, 'tgt', right)  3.23 us
  transfers between devices with their start and end apart: 15, of which 14 were waited for; matrix products, arithmetic and copies ran while one was open for 7% of the time, Pallas kernels for 0%

profile of v1, /device:TPU:0, one launch (start us, length us, event | category | flops | bytes accessed | tf_op | source)
XLA Modules:
  0.0 137.3 jit_solution(17632366642363668602)
XLA Ops:
  0.7 1.0 constant_dynamic-update-slice_fusion.16
  2.3 2.6 %fusion.17 = f32[2048,256]{1,0:T(8,128)} fusion(bf16[2048,128]{1,0:T(8,128)(2,1)S(1)} %bitcast.40, bf16[128,256]{1,0:T(8,128)(2,1)} %param.8, f32[256]{0:T(256)} %param.9), kind=kOutput, calls=%fused_computation.21 | convolution fusion | flops 135790592 | bytes 2688000 | tf_op jit(solution)/shard_map/dot_general | solution.py:9
  4.9 3.5 %reshape.38 = f32[4,2,128,2,256]{4,3,2,1,0:T(2,128)} reshape(f32[2048,256]{1,0:T(8,128)} %fusion.17) | data formatting | bytes 4194304 | tf_op jit(solution)/shard_map/reshape;reshape | solution.py:15
  8.3 3.1 %reduce_sum.27 = f32[4,128,256]{2,1,0:T(8,128)S(1)} reduce(f32[4,2,128,2,256]{4,3,2,1,0:T(2,128)} %reshape.38, f32[]{:T(128)} %constant.173.clone.1), dimensions={1,3}, to_apply=%region_0.0 | reduce | flops 393216 | bytes 2621444 | tf_op jit(solution)/shard_map/reduce_sum | solution.py:15
  12.6 2.7 %collective-permute-start.1 = (bf16[128,256]{1,0:T(8,128)(2,1)S(1)}, bf16[128,256]{1,0:T(8,128)(2,1)S(1)}, u32[]{:S(2)}, u32[]{:S(2)}) collective-permute-start(bf16[128,256]{1,0:T(8,128)(2,1)S(1)} %collective-permute-done), channel_id=1, source_target_pairs={{0,1},{1,2},{2,3},{3,4},{4,5},{5,6},{6,7},{7,8},{8,9},{9,10},{10,1... | collective-permute-start | bytes 196616 | tf_op jit(solution)/shard_map/ppermute | solution.py:55
  15.3 4.3 %collective-permute-done.1 = bf16[128,256]{1,0:T(8,128)(2,1)S(1)} collective-permute-done((bf16[128,256]{1,0:T(8,128)(2,1)S(1)}, bf16[128,256]{1,0:T(8,128)(2,1)S(1)}, u32[]{:S(2)}, u32[]{:S(2)}) %collective-permute-start.1) | collective-permute-done | bytes 65568 | tf_op jit(solution)/shard_map/ppermute | solution.py:55
  19.7 6.4 %collective-permute-done.2 = bf16[128,256]{1,0:T(8,128)(2,1)S(1)} collective-permute-done((bf16[128,256]{1,0:T(8,128)(2,1)S(1)}, bf16[128,256]{1,0:T(8,128)(2,1)S(1)}, u32[]{:S(2)}, u32[]{:S(2)}) %collective-permute-start.2) | collective-permute-done | bytes 65568 | tf_op jit(solution)/shard_map/ppermute | solution.py:55
  26.0 6.4 %collective-permute-done.3 = bf16[128,256]{1,0:T(8,128)(2,1)S(1)} collective-permute-done((bf16[128,256]{1,0:T(8,128)(2,1)S(1)}, bf16[128,256]{1,0:T(8,128)(2,1)S(1)}, u32[]{:S(2)}, u32[]{:S(2)}) %collective-permute-start.3) | collective-permute-done | bytes 65568 | tf_op jit(solution)/shard_map/ppermute | solution.py:55
  32.4 6.4 %collective-permute-done.4 = bf16[128,256]{1,0:T(8,128)(2,1)S(1)} collective-permute-done((bf16[128,256]{1,0:T(8,128)(2,1)S(1)}, bf16[128,256]{1,0:T(8,128)(2,1)S(1)}, u32[]{:S(2)}, u32[]{:S(2)}) %collective-permute-start.4) | collective-permute-done | bytes 65568 | tf_op jit(solution)/shard_map/ppermute | solution.py:55
  38.8 6.4 %collective-permute-done.5 = bf16[128,256]{1,0:T(8,128)(2,1)S(1)} collective-permute-done((bf16[128,256]{1,0:T(8,128)(2,1)S(1)}, bf16[128,256]{1,0:T(8,128)(2,1)S(1)}, u32[]{:S(2)}, u32[]{:S(2)}) %collective-permute-start.5) | collective-permute-done | bytes 65568 | tf_op jit(solution)/shard_map/ppermute | solution.py:55
  45.2 6.4 %collective-permute-done.6 = bf16[128,256]{1,0:T(8,128)(2,1)S(1)} collective-permute-done((bf16[128,256]{1,0:T(8,128)(2,1)S(1)}, bf16[128,256]{1,0:T(8,128)(2,1)S(1)}, u32[]{:S(2)}, u32[]{:S(2)}) %collective-permute-start.6) | collective-permute-done | bytes 65568 | tf_op jit(solution)/shard_map/ppermute | solution.py:55
  51.6 6.4 %collective-permute-done.7 = bf16[128,256]{1,0:T(8,128)(2,1)S(1)} collective-permute-done((bf16[128,256]{1,0:T(8,128)(2,1)S(1)}, bf16[128,256]{1,0:T(8,128)(2,1)S(1)}, u32[]{:S(2)}, u32[]{:S(2)}) %collective-permute-start.7) | collective-permute-done | bytes 65568 | tf_op jit(solution)/shard_map/ppermute | solution.py:55
  58.0 6.4 %collective-permute-done.8 = bf16[128,256]{1,0:T(8,128)(2,1)S(1)} collective-permute-done((bf16[128,256]{1,0:T(8,128)(2,1)S(1)}, bf16[128,256]{1,0:T(8,128)(2,1)S(1)}, u32[]{:S(2)}, u32[]{:S(2)}) %collective-permute-start.8) | collective-permute-done | bytes 65568 | tf_op jit(solution)/shard_map/ppermute | solution.py:55
  64.4 6.4 %collective-permute-done.9 = bf16[128,256]{1,0:T(8,128)(2,1)S(1)} collective-permute-done((bf16[128,256]{1,0:T(8,128)(2,1)S(1)}, bf16[128,256]{1,0:T(8,128)(2,1)S(1)}, u32[]{:S(2)}, u32[]{:S(2)}) %collective-permute-start.9) | collective-permute-done | bytes 65568 | tf_op jit(solution)/shard_map/ppermute | solution.py:55
  70.8 6.4 %collective-permute-done.10 = bf16[128,256]{1,0:T(8,128)(2,1)S(1)} collective-permute-done((bf16[128,256]{1,0:T(8,128)(2,1)S(1)}, bf16[128,256]{1,0:T(8,128)(2,1)S(1)}, u32[]{:S(2)}, u32[]{:S(2)}) %collective-permute-start.10) | collective-permute-done | bytes 65568 | tf_op jit(solution)/shard_map/ppermute | solution.py:55
  77.1 6.4 %collective-permute-done.11 = bf16[128,256]{1,0:T(8,128)(2,1)S(1)} collective-permute-done((bf16[128,256]{1,0:T(8,128)(2,1)S(1)}, bf16[128,256]{1,0:T(8,128)(2,1)S(1)}, u32[]{:S(2)}, u32[]{:S(2)}) %collective-permute-start.11) | collective-permute-done | bytes 65568 | tf_op jit(solution)/shard_map/ppermute | solution.py:55
  83.5 6.4 %collective-permute-done.12 = bf16[128,256]{1,0:T(8,128)(2,1)S(1)} collective-permute-done((bf16[128,256]{1,0:T(8,128)(2,1)S(1)}, bf16[128,256]{1,0:T(8,128)(2,1)S(1)}, u32[]{:S(2)}, u32[]{:S(2)}) %collective-permute-start.12) | collective-permute-done | bytes 65568 | tf_op jit(solution)/shard_map/ppermute | solution.py:55
  89.9 6.4 %collective-permute-done.13 = bf16[128,256]{1,0:T(8,128)(2,1)S(1)} collective-permute-done((bf16[128,256]{1,0:T(8,128)(2,1)S(1)}, bf16[128,256]{1,0:T(8,128)(2,1)S(1)}, u32[]{:S(2)}, u32[]{:S(2)}) %collective-permute-start.13) | collective-permute-done | bytes 65568 | tf_op jit(solution)/shard_map/ppermute | solution.py:55
  96.3 6.4 %collective-permute-done.14 = bf16[128,256]{1,0:T(8,128)(2,1)S(1)} collective-permute-done((bf16[128,256]{1,0:T(8,128)(2,1)S(1)}, bf16[128,256]{1,0:T(8,128)(2,1)S(1)}, u32[]{:S(2)}, u32[]{:S(2)}) %collective-permute-start.14) | collective-permute-done | bytes 65568 | tf_op jit(solution)/shard_map/ppermute | solution.py:55
  102.7 0.9 broadcast_in_dim.12
  103.6 1.6 %broadcast_in_dim.11.clone = bf16[512,2048]{1,0:T(8,128)(2,1)} broadcast(bf16[]{:T(256)} %constant.152.clone.1), dimensions={} | broadcast | bytes 2097154 | tf_op jit(solution)/shard_map/broadcast_in_dim | solution.py:62
  105.1 11.4 %while.15 = (s32[]{:T(128)}, bf16[512,2048]{1,0:T(8,128)(2,1)}, bf16[2048,128]{1,0:T(8,128)(2,1)}, bf16[2048,256]{1,0:T(8,128)(2,1)S(1)}, bf16[512,256]{1,0:T(8,...) while((s32[]{:T(128)}, bf16[512,2048]{1,0:T(8,128)(2,1)}, ...), condition=%wide.region_3.4_spmd, body=%wide.region_2.3_spmd.sunk | while | flops 336527360 | bytes 7079091 | solution.py:92
  105.4 0.9 fusion.52
  107.1 0.8 constant_dynamic-update-slice_fusion.18
  108.2 0.9 fusion.52
  110.0 0.8 constant_dynamic-update-slice_fusion.18
  111.0 0.9 fusion.52
  112.8 0.8 constant_dynamic-update-slice_fusion.18
  113.9 0.9 fusion.52
  115.7 0.8 constant_dynamic-update-slice_fusion.18
  116.5 18.0 %all_to_all.19 = bf16[16,128,128]{2,1,0:T(8,128)(2,1)S(1)} all-to-all(bf16[16,128,128]{2,1,0:T(8,128)(2,1)} %bitcast.5), channel_id=1, replica_groups=mesh['pairs'=2,'tgt'=16] {'tgt'}, dimensions={0} | all-to-all | bytes 1048576 | tf_op jit(solution)/shard_map/all_to_all | solution.py:94
  134.8 1.0 copy.25
  (62 shorter events, 7.7 us)
Async XLA Ops:
  0.6 1.7 %copy-start = (bf16[8,256,128]{2,1,0:T(8,128)(2,1)S(1)}, bf16[8,256,128]{2,1,0:T(8,128)(2,1)}, u32[]{:S(2)}) copy-start(bf16[8,256,128]{2,1,0:T(8,128)(2,1)} %param.7) | copy-start | bytes 1572868
  1.8 10.8 %collective-permute-start = (bf16[128,256]{1,0:T(8,128)(2,1)S(1)}, bf16[128,256]{1,0:T(8,128)(2,1)S(1)}, u32[]{:S(2)}, u32[]{:S(2)}) collective-permute-start(bf16[128,256]{1,0:T(8,128)(2,1)S(1)} %get-tuple-element.178), channel_id=1, source_target_pairs={{0,1},{1,2},{2,3},{3,4},{4,5},{5,6},{6,7},{7,8},{8,9},{9,10},{10,1... | collective-permute-start | bytes 196616 | tf_op jit(solution)/shard_map/ppermute | solution.py:55
  12.6 7.0 %collective-permute-start.1 = (bf16[128,256]{1,0:T(8,128)(2,1)S(1)}, bf16[128,256]{1,0:T(8,128)(2,1)S(1)}, u32[]{:S(2)}, u32[]{:S(2)}) collective-permute-start(bf16[128,256]{1,0:T(8,128)(2,1)S(1)} %collective-permute-done), channel_id=1, source_target_pairs={{0,1},{1,2},{2,3},{3,4},{4,5},{5,6},{6,7},{7,8},{8,9},{9,10},{10,1... | collective-permute-start | bytes 196616 | tf_op jit(solution)/shard_map/ppermute | solution.py:55
  19.6 6.4 %collective-permute-start.2 = (bf16[128,256]{1,0:T(8,128)(2,1)S(1)}, bf16[128,256]{1,0:T(8,128)(2,1)S(1)}, u32[]{:S(2)}, u32[]{:S(2)}) collective-permute-start(bf16[128,256]{1,0:T(8,128)(2,1)S(1)} %collective-permute-done.1), channel_id=1, source_target_pairs={{0,1},{1,2},{2,3},{3,4},{4,5},{5,6},{6,7},{7,8},{8,9},{9,10},{10,1... | collective-permute-start | bytes 196616 | tf_op jit(solution)/shard_map/ppermute | solution.py:55
  26.0 6.4 %collective-permute-start.3 = (bf16[128,256]{1,0:T(8,128)(2,1)S(1)}, bf16[128,256]{1,0:T(8,128)(2,1)S(1)}, u32[]{:S(2)}, u32[]{:S(2)}) collective-permute-start(bf16[128,256]{1,0:T(8,128)(2,1)S(1)} %collective-permute-done.2), channel_id=1, source_target_pairs={{0,1},{1,2},{2,3},{3,4},{4,5},{5,6},{6,7},{7,8},{8,9},{9,10},{10,1... | collective-permute-start | bytes 196616 | tf_op jit(solution)/shard_map/ppermute | solution.py:55
  32.4 6.4 %collective-permute-start.4 = (bf16[128,256]{1,0:T(8,128)(2,1)S(1)}, bf16[128,256]{1,0:T(8,128)(2,1)S(1)}, u32[]{:S(2)}, u32[]{:S(2)}) collective-permute-start(bf16[128,256]{1,0:T(8,128)(2,1)S(1)} %collective-permute-done.3), channel_id=1, source_target_pairs={{0,1},{1,2},{2,3},{3,4},{4,5},{5,6},{6,7},{7,8},{8,9},{9,10},{10,1... | collective-permute-start | bytes 196616 | tf_op jit(solution)/shard_map/ppermute | solution.py:55
  38.8 6.4 %collective-permute-start.5 = (bf16[128,256]{1,0:T(8,128)(2,1)S(1)}, bf16[128,256]{1,0:T(8,128)(2,1)S(1)}, u32[]{:S(2)}, u32[]{:S(2)}) collective-permute-start(bf16[128,256]{1,0:T(8,128)(2,1)S(1)} %collective-permute-done.4), channel_id=1, source_target_pairs={{0,1},{1,2},{2,3},{3,4},{4,5},{5,6},{6,7},{7,8},{8,9},{9,10},{10,1... | collective-permute-start | bytes 196616 | tf_op jit(solution)/shard_map/ppermute | solution.py:55
  45.2 6.4 %collective-permute-start.6 = (bf16[128,256]{1,0:T(8,128)(2,1)S(1)}, bf16[128,256]{1,0:T(8,128)(2,1)S(1)}, u32[]{:S(2)}, u32[]{:S(2)}) collective-permute-start(bf16[128,256]{1,0:T(8,128)(2,1)S(1)} %collective-permute-done.5), channel_id=1, source_target_pairs={{0,1},{1,2},{2,3},{3,4},{4,5},{5,6},{6,7},{7,8},{8,9},{9,10},{10,1... | collective-permute-start | bytes 196616 | tf_op jit(solution)/shard_map/ppermute | solution.py:55
  51.6 6.4 %collective-permute-start.7 = (bf16[128,256]{1,0:T(8,128)(2,1)S(1)}, bf16[128,256]{1,0:T(8,128)(2,1)S(1)}, u32[]{:S(2)}, u32[]{:S(2)}) collective-permute-start(bf16[128,256]{1,0:T(8,128)(2,1)S(1)} %collective-permute-done.6), channel_id=1, source_target_pairs={{0,1},{1,2},{2,3},{3,4},{4,5},{5,6},{6,7},{7,8},{8,9},{9,10},{10,1... | collective-permute-start | bytes 196616 | tf_op jit(solution)/shard_map/ppermute | solution.py:55
  58.0 6.4 %collective-permute-start.8 = (bf16[128,256]{1,0:T(8,128)(2,1)S(1)}, bf16[128,256]{1,0:T(8,128)(2,1)S(1)}, u32[]{:S(2)}, u32[]{:S(2)}) collective-permute-start(bf16[128,256]{1,0:T(8,128)(2,1)S(1)} %collective-permute-done.7), channel_id=1, source_target_pairs={{0,1},{1,2},{2,3},{3,4},{4,5},{5,6},{6,7},{7,8},{8,9},{9,10},{10,1... | collective-permute-start | bytes 196616 | tf_op jit(solution)/shard_map/ppermute | solution.py:55
  64.4 6.4 %collective-permute-start.9 = (bf16[128,256]{1,0:T(8,128)(2,1)S(1)}, bf16[128,256]{1,0:T(8,128)(2,1)S(1)}, u32[]{:S(2)}, u32[]{:S(2)}) collective-permute-start(bf16[128,256]{1,0:T(8,128)(2,1)S(1)} %collective-permute-done.8), channel_id=1, source_target_pairs={{0,1},{1,2},{2,3},{3,4},{4,5},{5,6},{6,7},{7,8},{8,9},{9,10},{10,1... | collective-permute-start | bytes 196616 | tf_op jit(solution)/shard_map/ppermute | solution.py:55
  70.7 6.4 %collective-permute-start.10 = (bf16[128,256]{1,0:T(8,128)(2,1)S(1)}, bf16[128,256]{1,0:T(8,128)(2,1)S(1)}, u32[]{:S(2)}, u32[]{:S(2)}) collective-permute-start(bf16[128,256]{1,0:T(8,128)(2,1)S(1)} %collective-permute-done.9), channel_id=1, source_target_pairs={{0,1},{1,2},{2,3},{3,4},{4,5},{5,6},{6,7},{7,8},{8,9},{9,10},{10,1... | collective-permute-start | bytes 196616 | tf_op jit(solution)/shard_map/ppermute | solution.py:55
  77.1 6.4 %collective-permute-start.11 = (bf16[128,256]{1,0:T(8,128)(2,1)S(1)}, bf16[128,256]{1,0:T(8,128)(2,1)S(1)}, u32[]{:S(2)}, u32[]{:S(2)}) collective-permute-start(bf16[128,256]{1,0:T(8,128)(2,1)S(1)} %collective-permute-done.10), channel_id=1, source_target_pairs={{0,1},{1,2},{2,3},{3,4},{4,5},{5,6},{6,7},{7,8},{8,9},{9,10},{10,1... | collective-permute-start | bytes 196616 | tf_op jit(solution)/shard_map/ppermute | solution.py:55
  83.5 6.4 %collective-permute-start.12 = (bf16[128,256]{1,0:T(8,128)(2,1)S(1)}, bf16[128,256]{1,0:T(8,128)(2,1)S(1)}, u32[]{:S(2)}, u32[]{:S(2)}) collective-permute-start(bf16[128,256]{1,0:T(8,128)(2,1)S(1)} %collective-permute-done.11), channel_id=1, source_target_pairs={{0,1},{1,2},{2,3},{3,4},{4,5},{5,6},{6,7},{7,8},{8,9},{9,10},{10,1... | collective-permute-start | bytes 196616 | tf_op jit(solution)/shard_map/ppermute | solution.py:55
  89.9 6.4 %collective-permute-start.13 = (bf16[128,256]{1,0:T(8,128)(2,1)S(1)}, bf16[128,256]{1,0:T(8,128)(2,1)S(1)}, u32[]{:S(2)}, u32[]{:S(2)}) collective-permute-start(bf16[128,256]{1,0:T(8,128)(2,1)S(1)} %collective-permute-done.12), channel_id=1, source_target_pairs={{0,1},{1,2},{2,3},{3,4},{4,5},{5,6},{6,7},{7,8},{8,9},{9,10},{10,1... | collective-permute-start | bytes 196616 | tf_op jit(solution)/shard_map/ppermute | solution.py:55
  96.3 6.4 %collective-permute-start.14 = (bf16[128,256]{1,0:T(8,128)(2,1)S(1)}, bf16[128,256]{1,0:T(8,128)(2,1)S(1)}, u32[]{:S(2)}, u32[]{:S(2)}) collective-permute-start(bf16[128,256]{1,0:T(8,128)(2,1)S(1)} %collective-permute-done.13), channel_id=1, source_target_pairs={{0,1},{1,2},{2,3},{3,4},{4,5},{5,6},{6,7},{7,8},{8,9},{9,10},{10,1... | collective-permute-start | bytes 196616 | tf_op jit(solution)/shard_map/ppermute | solution.py:55
